TPU v7x, 32 devices: a whole 2x2x4 slice. The times are simulated.
32 devices in a mesh: groups: 2 (over y), fsdp: 4 (over x, core), tensor: 4 (over z).
Axes of the slice: x: 2, y: 2, z: 4, core: 2. Of those that a mesh axis runs over, the one named last changes fastest.
Arguments:
- video: bfloat16 [8, 256, 3072], P(('groups', 'fsdp'), 'tensor'), parts along dimension 0, may hold values from -6 to 6
- timesteps: int32 [8, 3], P(('groups', 'fsdp')), parts along dimension 0, may hold values from 1 to 999
- text_keys: bfloat16 [8, 256, 512], P(('groups', 'fsdp'), None, 'tensor'), parts along dimension 0, may hold values from -490 to 490
- text_values: bfloat16 [8, 256, 512], P(('groups', 'fsdp'), None, 'tensor'), parts along dimension 0, may hold values from -6 to 6
- text_lengths: int32 [8], P(('groups', 'fsdp')), parts along dimension 0, may hold values from 64 to 256, as said below
- base_weights: bfloat16 [4, 3072, 512], P(None, None, 'tensor'), may hold values from -0.109375 to 0.109375
- delta_values: bfloat16 [4, 3072, 512], P(None, ('fsdp', 'tensor')), may hold values from -6 to 6
- delta_scales: float32 [4, 24, 4], replicated, may hold values from 0.002 to 0.02
- q_gain: float32 [128], replicated, may hold values from 1 to 2
- k_gain: float32 [128], replicated, may hold values from 1 to 2
- mod_weight: bfloat16 [256, 6, 3072], P(None, None, 'tensor'), may hold values from -0.75 to 0.75
- fc_in: bfloat16 [3072, 2560], P(None, 'tensor'), may hold values from -0.109375 to 0.109375
- fc_out: bfloat16 [2560, 3072], P('tensor'), may hold values from -0.125 to 0.125
Outputs:
- latent: bfloat16 [8, 256, 3072], P(('groups', 'fsdp'), 'tensor'), parts along dimension 0
- velocity: bfloat16 [8, 2, 256, 3072], P(('groups', 'fsdp'), None, 'tensor'), parts along dimension 0
There are 2 independent parts, one for each index of `groups`. A program takes and returns all parts, laid end to end along the dimension named above; an argument that names none is the same for every part. Nothing has to cross between parts.
Inputs may be any that keep to these rules, and one draw needn't show every extreme that they name: `text_lengths`: each sample's number of valid text tokens.
All inputs are finite; a program needn't handle non-finite values.
Results may differ from a plain program's by a relative error of at most 0.038.
Values may be sent and summed in bfloat16 or wider, within the bound.
A program may use at most 64 MiB of HBM per device.

v0:
```python
import math

import jax
import jax.numpy as jnp
from jax import lax
from jax.sharding import PartitionSpec as P

STEPS = 2


def layer_norm(values):
    center = values - jnp.mean(values, axis=-1, keepdims=True)
    spread = jnp.mean(center * center, axis=-1, keepdims=True)
    return center * lax.rsqrt(spread + 1e-06)


def rms_scale(values, gain):
    power = jnp.mean(values * values, axis=-1, keepdims=True)
    return values * lax.rsqrt(power + 1e-06) * gain


def time_embed(times, freq_count):
    half_count = freq_count // 2
    ladder = jnp.exp(-math.log(10000.0) * jnp.arange(half_count, dtype=jnp.float32) / half_count)
    angles = times.astype(jnp.float32)[:, None] * ladder[None, :]
    return jnp.concatenate([jnp.cos(angles), jnp.sin(angles)], axis=1)


def shards(
    video,
    timesteps,
    text_keys,
    text_values,
    text_lengths,
    base_weights,
    delta_values,
    delta_scales,
    q_gain,
    k_gain,
    mod_weight,
    fc_in,
    fc_out,
):
    head_dim = q_gain.shape[0]
    head_width = base_weights.shape[2]
    heads_here = head_width // head_dim
    text_count = text_keys.shape[1]
    column_index = lax.axis_index("tensor")
    embedding = jax.nn.silu(time_embed(timesteps[0, :STEPS], mod_weight.shape[0])).astype(
        jnp.bfloat16
    )
    mod_part = jnp.einsum("sf,fkd->skd", embedding, mod_weight, preferred_element_type=jnp.float32)
    modulation = lax.all_gather(mod_part, "tensor", axis=2, tiled=True)
    block_rows = lax.all_gather(delta_values, "tensor", axis=1, tiled=True)
    own_delta = lax.dynamic_slice_in_dim(block_rows, column_index * head_width, head_width, 2)
    own_scales = lax.dynamic_slice_in_dim(delta_scales, column_index * heads_here, heads_here, 2)
    row_scales = jnp.repeat(own_scales, head_dim, axis=1)
    dequantize_piece = lax.all_gather(own_delta, "fsdp", axis=1, tiled=True)
    scale_full = jnp.repeat(row_scales, head_dim, axis=2)
    weights = (
        base_weights.astype(jnp.float32) + dequantize_piece.astype(jnp.float32) * scale_full
    ).astype(jnp.bfloat16)
    qkv_weights = weights[:3]
    out_weight = weights[3]
    latent = video[0].astype(jnp.float32)
    text_valid = jnp.arange(text_count) < text_lengths[0]
    text_k = text_keys[0]
    text_v = text_values[0]
    velocities = []
    for step in range(STEPS):
        mods = modulation[step]
        attn_in = (layer_norm(latent) * (1.0 + mods[1]) + mods[0]).astype(jnp.bfloat16)
        piece = lax.all_gather(attn_in, "tensor", axis=0, tiled=True)
        count = piece.shape[0]
        joined = jnp.einsum("rd,kdc->rkc", piece, qkv_weights, preferred_element_type=jnp.float32)
        query = rms_scale(joined[:, 0].reshape(count, heads_here, head_dim), q_gain).reshape(
            count, head_width
        )
        key_part = rms_scale(joined[:, 1].reshape(count, heads_here, head_dim), k_gain).reshape(
            count, head_width
        )
        projected = jnp.stack([query, key_part, joined[:, 2]], axis=1).astype(jnp.bfloat16)
        video_count = projected.shape[0]
        query = projected[:, 0].reshape(video_count, heads_here, head_dim)
        all_keys = jnp.concatenate([projected[:, 1], text_k], axis=0).reshape(
            -1, heads_here, head_dim
        )
        all_values = jnp.concatenate([projected[:, 2], text_v], axis=0).reshape(
            -1, heads_here, head_dim
        )
        key_valid = jnp.concatenate([jnp.ones((video_count,), dtype=bool), text_valid])
        scores = jnp.einsum(
            "qhd,khd->hqk", query, all_keys, preferred_element_type=jnp.float32
        ) / math.sqrt(head_dim)
        scores = jnp.where(key_valid[None, None, :], scores, -jnp.inf)
        soft = jax.nn.softmax(scores, axis=-1).astype(jnp.bfloat16)
        mixed = jnp.einsum(
            "hqk,khd->qhd", soft, all_values, preferred_element_type=jnp.float32
        ).astype(jnp.bfloat16)
        mixed = mixed.reshape(video_count, head_width)
        attn = lax.psum_scatter(
            lax.dot_general(
                mixed, out_weight, (((1,), (1,)), ((), ())), preferred_element_type=jnp.float32
            ).astype(jnp.bfloat16),
            "tensor",
            scatter_dimension=0,
            tiled=True,
        ).astype(jnp.float32)
        midway = latent + mods[2] * attn
        mlp_in = (layer_norm(midway) * (1.0 + mods[4]) + mods[3]).astype(jnp.bfloat16)
        hidden = jax.nn.gelu(
            jnp.dot(
                lax.all_gather(mlp_in, "tensor", axis=0, tiled=True),
                fc_in,
                preferred_element_type=jnp.float32,
            ),
            approximate=True,
        ).astype(jnp.bfloat16)
        mlp = lax.psum_scatter(
            jnp.dot(hidden, fc_out, preferred_element_type=jnp.float32).astype(jnp.bfloat16),
            "tensor",
            scatter_dimension=0,
            tiled=True,
        ).astype(jnp.float32)
        update = mods[2] * attn + mods[5] * mlp
        velocities.append(update.astype(jnp.bfloat16))
        step_size = (timesteps[0, step + 1] - timesteps[0, step]).astype(jnp.float32) / 1000.0
        latent = latent + step_size * update
    return (latent.astype(jnp.bfloat16)[None], jnp.stack(velocities)[None])


def solution(mesh):
    in_specs = (
        P(("groups", "fsdp"), "tensor", None),
        P(("groups", "fsdp"), None),
        P(("groups", "fsdp"), None, "tensor"),
        P(("groups", "fsdp"), None, "tensor"),
        P(("groups", "fsdp")),
        P(None, None, "tensor"),
        P(None, ("fsdp", "tensor"), None),
        P(),
        P(),
        P(),
        P(None, None, "tensor"),
        P(None, "tensor"),
        P("tensor", None),
    )
    out_specs = (P(("groups", "fsdp"), "tensor", None), P(("groups", "fsdp"), None, "tensor", None))
    return jax.shard_map(shards, mesh=mesh, in_specs=in_specs, out_specs=out_specs, check_vma=False)
```

profile of v0, /device:TPU:0, one launch (start us, length us, event | category | flops | bytes accessed | tf_op | source)
XLA Modules:
  0.0 447.8 jit_solution(14852415099114301194)
XLA Ops:
  7.2 0.0 all-gather.9.cloned.1.call-start
  7.2 0.7 all-gather.9.cloned.1.call-update
  7.9 0.0 all-gather.11.cloned.1.call-start
  8.0 67.8 %all-gather.9.cloned.1.call-done = bf16[4,768,512]{2,1,0:T(8,128)(2,1)} async-done(((bf16[4,192,512]{2,1,0:T(8,128)(2,1)}), bf16[4,768,512]{2,1,0:T(8,128)(2,1)}) %all-gather.9.cloned.1.call-update) | async-done | bytes 3145744 | tf_op jit(solution)/shard_map/all_gather | solution.py:54
  75.8 2.1 constant_dynamic-slice_fusion.1
  77.9 0.0 all-gather.11.cloned.1.call-update
  77.9 0.0 all-gather.7.cloned.1.call-start
  78.0 0.1 multiply_cosine_fusion
  78.1 0.4 fusion.82
  78.5 13.6 %all_gather.21 = f32[2,6,3072]{2,0,1:T(2,128)S(1)} all-gather(f32[2,6,768]{2,0,1:T(2,128)S(1)} %fusion.82), channel_id=1, replica_groups=mesh['groups'=2,'fsdp'=4,'tensor'=4] {'tensor'}, dimensions={2}, use_global_device_ids=true | all-gather | bytes 184320 | tf_op jit(solution)/shard_map/all_gather | solution.py:53
  92.1 0.2 convert_reduce_fusion
  92.2 0.3 fusion.15
  92.5 0.7 fusion.103
  93.3 1.0 fusion.18
  94.2 0.0 all-gather.7.cloned.1.call-update
  94.2 0.0 reduce-scatter.5.cloned.1.call-start
  94.3 0.7 constant_dynamic-slice_fusion
  95.0 0.1 broadcast_bitcast_fusion
  95.8 9.5 %all-gather.11.cloned.1.call-done = bf16[4,3072,128]{2,1,0:T(8,128)(2,1)} async-done(((bf16[4,768,128]{2,1,0:T(8,128)(2,1)}), bf16[4,3072,128]{2,1,0:T(8,128)(2,1)}) %all-gather.11.cloned.1.call-update) | async-done | bytes 3145744 | tf_op jit(solution)/shard_map/all_gather | solution.py:58
  105.3 6.1 %add_convert_fusion = bf16[4,3072,128]{2,1,0:T(8,128)(2,1)} fusion(bf16[4,3072,128]{2,1,0:T(8,128)(2,1)} %all-gather.11.cloned.1.call-done, bf16[4,3072,128]{2,1,0:T(8,128)(2,1)} %param.18, f32[4,3072]{1,0:T(4,128)S(1)} %bitcast.123), kind=kLoop, calls=%fused_computation | loop fusion | flops 7864320 | bytes 9486336 | tf_op jit(solution)/shard_map/convert_element_type | solution.py:62
  111.4 33.2 %all-gather.7.cloned.1.call-done = bf16[256,3072]{1,0:T(8,128)(2,1)} async-done(((bf16[64,3072]{1,0:T(8,128)(2,1)}), bf16[256,3072]{1,0:T(8,128)(2,1)}) %all-gather.7.cloned.1.call-update) | async-done | bytes 1572880 | tf_op jit(solution)/shard_map/all_gather | solution.py:73
  144.5 3.1 fusion.2
  147.7 0.1 multiply_reduce_fusion.6
  147.9 0.1 fusion.71
  148.0 0.4 fusion.105
  148.4 0.8 copy-done.4
  149.1 0.2 fusion.39
  149.4 3.5 convolution_convert_fusion.3
  152.8 0.0 reduce-scatter.5.cloned.1.call-update
  152.8 0.0 all-gather.13.cloned.1.call-start
  152.9 34.2 %reduce-scatter.5.cloned.1.call-done = bf16[64,3072]{1,0:T(8,128)(2,1)} async-done(((bf16[256,3072]{1,0:T(8,128)(2,1)}), bf16[64,3072]{1,0:T(8,128)(2,1)}) %reduce-scatter.5.cloned.1.call-update) | async-done | bytes 393232 | tf_op jit(solution)/shard_map/reduce_scatter | solution.py:101
  187.1 1.2 fusion.38
  188.4 1.3 multiply_reduce_fusion.2
  189.7 2.0 add_convert_fusion.4
  191.7 0.0 reduce-scatter.7.cloned.1.call-start
  191.7 36.2 %all-gather.13.cloned.1.call-done = bf16[256,3072]{1,0:T(8,128)(2,1)} async-done(((bf16[64,3072]{1,0:T(8,128)(2,1)}), bf16[256,3072]{1,0:T(8,128)(2,1)}) %all-gather.13.cloned.1.call-update) | async-done | bytes 1572880 | tf_op jit(solution)/shard_map/all_gather | solution.py:113
  227.9 7.6 %convolution_convert_fusion.1 = bf16[256,3072]{1,0:T(8,128)(2,1)} fusion(bf16[640,3072]{1,0:T(8,128)(2,1)} %param.25, bf16[256,3072]{1,0:T(8,128)(2,1)} %all-gather.13.cloned.1.call-done, bf16[3072,640]{1,0:T(8,128)(2,1)} %param.24), kind=kOutput, calls=%fused_computation.2 | convolution fusion | flops 2015526912 | bytes 11010048 | tf_op jit(solution)/shard_map/dot_general | solution.py:120
  235.5 0.0 all-gather.15.cloned.1.call-start
  235.6 0.7 fusion.104
  237.6 32.3 %reduce-scatter.7.cloned.1.call-done = bf16[64,3072]{1,0:T(8,128)(2,1)} async-done(((bf16[256,3072]{1,0:T(8,128)(2,1)}), bf16[64,3072]{1,0:T(8,128)(2,1)}) %reduce-scatter.7.cloned.1.call-update) | async-done | bytes 393232 | tf_op jit(solution)/shard_map/reduce_scatter | solution.py:119
  269.8 2.2 fusion.101
  272.1 0.3 multiply_reduce_fusion.1
  272.3 1.7 add_convert_fusion.3
  274.0 0.0 reduce-scatter.9.cloned.1.call-start
  274.1 36.2 %all-gather.15.cloned.1.call-done = bf16[256,3072]{1,0:T(8,128)(2,1)} async-done(((bf16[64,3072]{1,0:T(8,128)(2,1)}), bf16[256,3072]{1,0:T(8,128)(2,1)}) %all-gather.15.cloned.1.call-update) | async-done | bytes 1572880 | tf_op jit(solution)/shard_map/all_gather | solution.py:73
  310.3 3.1 fusion
  313.4 0.1 multiply_reduce_fusion.4
  313.5 0.6 fusion.76
  314.2 0.1 fusion.74
  314.3 1.2 fusion.106
  315.5 0.8 copy-done.3
  316.3 0.2 fusion.40
  316.5 3.5 convolution_convert_fusion.2
  320.1 0.0 all-gather.17.cloned.1.call-start
  320.2 34.3 %reduce-scatter.9.cloned.1.call-done = bf16[64,3072]{1,0:T(8,128)(2,1)} async-done(((bf16[256,3072]{1,0:T(8,128)(2,1)}), bf16[64,3072]{1,0:T(8,128)(2,1)}) %reduce-scatter.9.cloned.1.call-update) | async-done | bytes 393232 | tf_op jit(solution)/shard_map/reduce_scatter | solution.py:101
  354.4 1.2 fusion.62
  355.6 1.3 multiply_reduce_fusion
  356.9 2.0 add_convert_fusion.2
  358.9 0.2 reduce-scatter.11.cloned.1.call-start
  359.2 36.0 %all-gather.17.cloned.1.call-done = bf16[256,3072]{1,0:T(8,128)(2,1)} async-done(((bf16[64,3072]{1,0:T(8,128)(2,1)}), bf16[256,3072]{1,0:T(8,128)(2,1)}) %all-gather.17.cloned.1.call-update) | async-done | bytes 1572880 | tf_op jit(solution)/shard_map/all_gather | solution.py:113
  395.1 7.6 %convolution_convert_fusion = bf16[256,3072]{1,0:T(8,128)(2,1)} fusion(bf16[640,3072]{1,0:T(8,128)(2,1)} %param.25, bf16[256,3072]{1,0:T(8,128)(2,1)} %all-gather.17.cloned.1.call-done, bf16[3072,640]{1,0:T(8,128)(2,1)} %param.24), kind=kOutput, calls=%fused_computation.1 | convolution fusion | flops 2015526912 | bytes 11010048 | tf_op jit(solution)/shard_map/dot_general | solution.py:120
  404.0 33.1 %reduce-scatter.11.cloned.1.call-done = bf16[64,3072]{1,0:T(8,128)(2,1)} async-done(((bf16[256,3072]{1,0:T(8,128)(2,1)}), bf16[64,3072]{1,0:T(8,128)(2,1)}) %reduce-scatter.11.cloned.1.call-update) | async-done | bytes 393232 | tf_op jit(solution)/shard_map/reduce_scatter | solution.py:119
  437.0 2.0 fusion.41
  439.0 1.9 maximum_bitcast_fusion
  (49 shorter events, 0.3 us)
Async XLA Ops:
  7.2 70.9 %copy-start = (bf16[256,6,768]{2,0,1:T(8,128)(2,1)S(1)}, bf16[256,6,768]{2,0,1:T(8,128)(2,1)}, u32[]{:S(2)}) copy-start(bf16[256,6,768]{2,0,1:T(8,128)(2,1)} %param.23) | copy-start | bytes 7077892
  7.2 70.8 %copy-start.8 = (s32[1,3]{1,0:T(1,128)S(1)}, s32[1,3]{1,0:T(1,128)}, u32[]{:S(2)}) copy-start(s32[1,3]{1,0:T(1,128)} %param.14) | copy-start | bytes 40
  7.2 84.9 %copy-start.1 = (bf16[1,64,3072]{2,1,0:T(8,128)(2,1)S(1)}, bf16[1,64,3072]{2,1,0:T(8,128)(2,1)}, u32[]{:S(2)}) copy-start(bf16[1,64,3072]{2,1,0:T(8,128)(2,1)} %param.13) | copy-start | bytes 1179652
  7.2 68.6 %all-gather.9.cloned.1.call-start = ((), (), s32[]{:S(2)}) async-start(), calls=%async_computation.5 | async-start | bytes 3932160 | tf_op jit(solution)/shard_map/all_gather | solution.py:54
  7.9 97.3 %all-gather.11.cloned.1.call-start = ((), (), s32[]{:S(2)}) async-start(), calls=%async_computation.6 | async-start | bytes 3932160 | tf_op jit(solution)/shard_map/all_gather | solution.py:58
  77.9 66.7 %all-gather.7.cloned.1.call-start = ((), (), s32[]{:S(2)}) async-start(), calls=%async_computation.4 | async-start | bytes 1966080 | tf_op jit(solution)/shard_map/all_gather | solution.py:73
  93.3 96.4 %copy-start.5 = (f32[1,1,3072]{2,0,1:T(1,128)}, f32[1,1,3072]{2,0,1:T(1,128)S(1)}, u32[]{:S(2)}) copy-start(f32[1,1,3072]{2,0,1:T(1,128)S(1)} %get-tuple-element.22) | copy-start | bytes 36868
  94.2 92.9 %reduce-scatter.5.cloned.1.call-start = ((), (), s32[]{:S(2)}) async-start(), calls=%async_computation.7 | async-start | bytes 1966080 | tf_op jit(solution)/shard_map/reduce_scatter | solution.py:101
  95.8 52.2 %copy-start.13 = (pred[512]{0:T(512)(128)(4,1)}, pred[512]{0:T(512)(128)(4,1)S(1)}, u32[]{:S(2)}) copy-start(pred[512]{0:T(512)(128)(4,1)S(1)} %concatenate.21) | copy-start | bytes 1540
  111.4 36.5 %copy-start.9 = (f32[128]{0:T(128)S(1)}, f32[128]{0:T(128)}, u32[]{:S(2)}) copy-start(f32[128]{0:T(128)} %param.22) | copy-start | bytes 1540
  111.4 36.6 %copy-start.10 = (bf16[1,256,128]{2,1,0:T(8,128)(2,1)S(1)}, bf16[1,256,128]{2,1,0:T(8,128)(2,1)}, u32[]{:S(2)}) copy-start(bf16[1,256,128]{2,1,0:T(8,128)(2,1)} %param.15) | copy-start | bytes 196612
  111.4 36.6 %copy-start.12 = (f32[128]{0:T(128)S(1)}, f32[128]{0:T(128)}, u32[]{:S(2)}) copy-start(f32[128]{0:T(128)} %param.21) | copy-start | bytes 1540
  111.4 38.0 %copy-start.11 = (bf16[1,256,128]{2,1,0:T(8,128)(2,1)S(1)}, bf16[1,256,128]{2,1,0:T(8,128)(2,1)}, u32[]{:S(2)}) copy-start(bf16[1,256,128]{2,1,0:T(8,128)(2,1)} %param.16) | copy-start | bytes 196612
  148.3 0.8 copy-start.4
  152.8 75.1 %all-gather.13.cloned.1.call-start = ((), (), s32[]{:S(2)}) async-start(), calls=%async_computation.8 | async-start | bytes 1966080 | tf_op jit(solution)/shard_map/all_gather | solution.py:113
  191.7 78.1 %reduce-scatter.7.cloned.1.call-start = ((), (), s32[]{:S(2)}) async-start(), calls=%async_computation.9 | async-start | bytes 1966080 | tf_op jit(solution)/shard_map/reduce_scatter | solution.py:119
  235.5 74.7 %all-gather.15.cloned.1.call-start = ((), (), s32[]{:S(2)}) async-start(), calls=%async_computation.10 | async-start | bytes 1966080 | tf_op jit(solution)/shard_map/all_gather | solution.py:73
  274.0 80.4 %reduce-scatter.9.cloned.1.call-start = ((), (), s32[]{:S(2)}) async-start(), calls=%async_computation.11 | async-start | bytes 1966080 | tf_op jit(solution)/shard_map/reduce_scatter | solution.py:101
  315.5 0.8 copy-start.3
  316.5 40.4 %copy-start.6 = (f32[1,1,3072]{2,0,1:T(1,128)S(1)}, f32[1,1,3072]{2,0,1:T(1,128)}, u32[]{:S(2)}) copy-start(f32[1,1,3072]{2,0,1:T(1,128)} %get-tuple-element.12) | copy-start | bytes 36868
  316.5 40.4 %copy-start.7 = (f32[1,1,3072]{2,0,1:T(1,128)S(1)}, f32[1,1,3072]{2,0,1:T(1,128)}, u32[]{:S(2)}) copy-start(f32[1,1,3072]{2,0,1:T(1,128)} %get-tuple-element.13) | copy-start | bytes 36868
  320.1 75.0 %all-gather.17.cloned.1.call-start = ((), (), s32[]{:S(2)}) async-start(), calls=%async_computation.12 | async-start | bytes 1966080 | tf_op jit(solution)/shard_map/all_gather | solution.py:113
  358.9 78.1 %copy-start.2 = (bf16[64,3072]{1,0:T(8,128)(2,1)S(1)}, bf16[64,3072]{1,0:T(8,128)(2,1)}, u32[]{:S(2)}) copy-start(bf16[64,3072]{1,0:T(8,128)(2,1)} %reduce-scatter.9.cloned.1.call-done) | copy-start | bytes 1179652
  358.9 78.1 %reduce-scatter.11.cloned.1.call-start = ((), (), s32[]{:S(2)}) async-start(), calls=%async_computation.13 | async-start | bytes 1966080 | tf_op jit(solution)/shard_map/reduce_scatter | solution.py:119
Sparse Core Ops, SparseCore 0:
  9.6 66.1 all-gather.8
  78.0 27.2 all-gather.10
  107.4 37.0 all-gather.6
  153.0 34.1 reduce-scatter.4
  191.8 36.0 all-gather.12
  235.6 34.1 reduce-scatter.6
  274.1 36.0 all-gather.14
  320.2 34.1 reduce-scatter.8
  359.1 36.0 all-gather.16
  402.9 34.1 reduce-scatter.10
where the time goes:
time: 449 us; the launch traced here: 448 us
  waiting for transfers between devices  353 us (79%)
  matrix products  30.4 us (7%)
  other arithmetic  26.3 us (6%)
  between operations  17.7 us (4%)
  blocking collectives  13.6 us (3%)
  local copies, waits for them, and re-layouts  5.81 us (1%)
    all_gather x2, waiting for transfers between devices, shards(): lax.all_gather(mlp_in, 'tensor', axis=0, tiled=True)  72.1 us
    all_gather x2, waiting for transfers between devices, shards(): piece = lax.all_gather(attn_in, 'tensor', axis=0, tiled=True)  69.3 us
    reduce_scatter x2, waiting for transfers between devices, shards(): lax.psum_scatter(lax.dot_general(mixed, out_weight, (((1,), (1,)), ((), (...  68.5 us
    all_gather x1, waiting for transfers between devices, shards(): block_rows = lax.all_gather(delta_values, 'tensor', axis=1, tiled=True)  67.8 us
    reduce_scatter x2, waiting for transfers between devices, shards(): lax.psum_scatter(jnp.dot(hidden, fc_out, preferred_element_type=jnp.float...  65.3 us
    dot_general x2, matrix products, shards(): jnp.dot(hidden, fc_out, preferred_element_type=jnp.float32)  15.2 us
    all_gather x1, blocking collectives, shards(): modulation = lax.all_gather(mod_part, 'tensor', axis=2, tiled=True)  13.6 us
    all_gather x1, waiting for transfers between devices, shards(): dequantize_piece = lax.all_gather(own_delta, 'fsdp', axis=1, tiled=True)  9.47 us
  transfers between devices with their start and end apart: 10, of which 10 were waited for; matrix products, arithmetic and copies ran while one was open for 2% of the time, Pallas kernels for 0%

commit v1 on v0

--- a/solution.py
+++ b/solution.py
@@ -1,8 +1,11 @@
+import functools
 import math
 
 import jax
 import jax.numpy as jnp
 from jax import lax
+from jax.experimental import pallas as pl
+from jax.experimental.pallas import tpu as pltpu
 from jax.sharding import PartitionSpec as P
 
 STEPS = 2
@@ -24,6 +27,323 @@
     ladder = jnp.exp(-math.log(10000.0) * jnp.arange(half_count, dtype=jnp.float32) / half_count)
     angles = times.astype(jnp.float32)[:, None] * ladder[None, :]
     return jnp.concatenate([jnp.cos(angles), jnp.sin(angles)], axis=1)
+
+
+def line_copy(src, dst, send_sem, recv_sem, target):
+    return pltpu.make_async_remote_copy(
+        src_ref=src,
+        dst_ref=dst,
+        send_sem=send_sem,
+        recv_sem=recv_sem,
+        device_id={"tensor": target},
+        device_id_type=pl.DeviceIdType.MESH,
+    )
+
+
+def greet_neighbours(z, n):
+    barrier = pltpu.get_barrier_semaphore()
+
+    @pl.when(z > 0)
+    def _():
+        pl.semaphore_signal(
+            barrier, inc=1, device_id={"tensor": z - 1}, device_id_type=pl.DeviceIdType.MESH
+        )
+
+    @pl.when(z < n - 1)
+    def _():
+        pl.semaphore_signal(
+            barrier, inc=1, device_id={"tensor": z + 1}, device_id_type=pl.DeviceIdType.MESH
+        )
+
+    pl.semaphore_wait(barrier, jnp.where(z > 0, 1, 0) + jnp.where(z < n - 1, 1, 0))
+
+
+class Gather:
+    def __init__(self, z, n, buf, send_sem, recv_sem):
+        self.z, self.n, self.buf, self.send_sem, self.recv_sem = z, n, buf, send_sem, recv_sem
+
+    def copy(self, c, owner, way):
+        block = self.buf.at[c, owner]
+        target = self.z + 1 if way == 0 else self.z - 1
+        return line_copy(
+            block, block, self.send_sem.at[way, c, owner], self.recv_sem.at[c, owner], target
+        )
+
+    def start(self, c):
+        z, n = self.z, self.n
+
+        @pl.when(z < n - 1)
+        def _():
+            self.copy(c, z, 0).start()
+
+        @pl.when(z > 0)
+        def _():
+            self.copy(c, z, 1).start()
+
+    def forward(self, c):
+        z, n = self.z, self.n
+        for d in range(1, n):
+
+            @pl.when(z - d >= 0)
+            def _():
+                self.copy(c, z - d, 0).wait_recv()
+
+                @pl.when(z < n - 1)
+                def _():
+                    self.copy(c, z - d, 0).start()
+
+            @pl.when(z + d <= n - 1)
+            def _():
+                self.copy(c, z + d, 1).wait_recv()
+
+                @pl.when(z > 0)
+                def _():
+                    self.copy(c, z + d, 1).start()
+
+    def finish(self, c):
+        z, n = self.z, self.n
+        for o in range(n):
+
+            @pl.when((z >= o) & (z < n - 1))
+            def _():
+                self.copy(c, o, 0).wait_send()
+
+            @pl.when((z <= o) & (z > 0))
+            def _():
+                self.copy(c, o, 1).wait_send()
+
+
+class Scatter:
+    def __init__(self, z, n, term, recv, send_sem, recv_sem):
+        self.z, self.n, self.term, self.recv = z, n, term, recv
+        self.send_sem, self.recv_sem = send_sem, recv_sem
+
+    def copy(self, c, o, way):
+        target = self.z + 1 if way == 0 else self.z - 1
+        return line_copy(
+            self.term.at[c, o],
+            self.recv.at[way, c, o],
+            self.send_sem.at[c, o],
+            self.recv_sem.at[way, c, o],
+            target,
+        )
+
+    def ends(self, c):
+        z, n = self.z, self.n
+        for k in range(n - 1):
+
+            @pl.when(z == 0)
+            def _():
+                self.copy(c, n - 1 - k, 0).start()
+
+            @pl.when(z == n - 1)
+            def _():
+                self.copy(c, k, 1).start()
+
+    def add(self, c, o, way):
+        self.copy(c, o, way).wait_recv()
+        total = self.term[c, o].astype(jnp.float32) + self.recv[way, c, o].astype(jnp.float32)
+        self.term[c, o] = total.astype(jnp.bfloat16)
+        self.copy(c, o, way).start()
+
+    def forward(self, c):
+        z, n = self.z, self.n
+        for k in range(n - 1):
+            right, left = n - 1 - k, k
+
+            @pl.when((z > 0) & (z < right))
+            def _():
+                self.add(c, right, 0)
+
+            @pl.when((z < n - 1) & (z > left))
+            def _():
+                self.add(c, left, 1)
+
+    def collect(self, c, total):
+        z, n = self.z, self.n
+        total[...] = self.term[c, z].astype(jnp.float32)
+
+        @pl.when(z > 0)
+        def _():
+            self.copy(c, z, 0).wait_recv()
+            total[...] += self.recv[0, c, z].astype(jnp.float32)
+
+        @pl.when(z < n - 1)
+        def _():
+            self.copy(c, z, 1).wait_recv()
+            total[...] += self.recv[1, c, z].astype(jnp.float32)
+
+    def finish(self, c):
+        z, n = self.z, self.n
+        for o in range(n):
+
+            @pl.when(z < o)
+            def _():
+                self.copy(c, o, 0).wait_send()
+
+            @pl.when(z > o)
+            def _():
+                self.copy(c, o, 1).wait_send()
+
+
+def tail_kernel(
+    n,
+    chunks,
+    last,
+    step_ref,
+    mixed_ref,
+    out_weight_ref,
+    latent_ref,
+    mods_ref,
+    next_ref,
+    fc_in_ref,
+    fc_out_ref,
+    new_ref,
+    velocity_ref,
+    gathered_ref,
+    attn_term,
+    attn_recv,
+    mlp_in_all,
+    mlp_term,
+    mlp_recv,
+    attn_sum,
+    total,
+    hidden_ref,
+    as_send,
+    as_recv,
+    mg_send,
+    mg_recv,
+    ms_send,
+    ms_recv,
+    ag_send,
+    ag_recv,
+):
+    z = lax.axis_index("tensor")
+    tokens, width = latent_ref.shape
+    rows = tokens // chunks
+    tile = math.gcd(width, 768)
+    attn_out = Scatter(z, n, attn_term, attn_recv, as_send, as_recv)
+    mlp_gather = Gather(z, n, mlp_in_all, mg_send, mg_recv)
+    mlp_out = Scatter(z, n, mlp_term, mlp_recv, ms_send, ms_recv)
+    next_gather = None if last else Gather(z, n, gathered_ref, ag_send, ag_recv)
+
+    greet_neighbours(z, n)
+    for c in range(chunks):
+        part = mixed_ref[c * n * rows : (c + 1) * n * rows, :]
+        for t in range(0, width, tile):
+            product = lax.dot_general(
+                part,
+                out_weight_ref[t : t + tile, :],
+                (((1,), (1,)), ((), ())),
+                preferred_element_type=jnp.float32,
+            ).astype(jnp.bfloat16)
+            attn_term[c, :, :, t : t + tile] = product.reshape(n, rows, tile)
+        attn_out.ends(c)
+
+    def after_attention(c):
+        attn_out.forward(c)
+        attn_out.collect(c, attn_sum.at[c])
+        own = slice(c * rows, (c + 1) * rows)
+        gated = mods_ref[2:3, :] * attn_sum[c]
+        midway = latent_ref[own, :] + gated
+        attn_sum[c] = gated
+        mlp_in = layer_norm(midway) * (1.0 + mods_ref[4:5, :]) + mods_ref[3:4, :]
+        mlp_in_all[c, z] = mlp_in.astype(jnp.bfloat16)
+        mlp_gather.start(c)
+
+    def feed_forward(c):
+        mlp_gather.forward(c)
+        tokens_in = mlp_in_all[c].reshape(n * rows, width)
+        hidden = jax.nn.gelu(
+            jnp.dot(tokens_in, fc_in_ref[...], preferred_element_type=jnp.float32),
+            approximate=True,
+        )
+        hidden_ref[...] = hidden.astype(jnp.bfloat16)
+        for t in range(0, width, tile):
+            product = jnp.dot(
+                hidden_ref[...], fc_out_ref[:, t : t + tile], preferred_element_type=jnp.float32
+            ).astype(jnp.bfloat16)
+            mlp_term[c, :, :, t : t + tile] = product.reshape(n, rows, tile)
+        mlp_out.ends(c)
+
+    def after_feed_forward(c):
+        mlp_out.forward(c)
+        mlp_out.collect(c, total)
+        own = slice(c * rows, (c + 1) * rows)
+        update = attn_sum[c] + mods_ref[5:6, :] * total[...]
+        velocity_ref[own, :] = update.astype(jnp.bfloat16)
+        fresh = latent_ref[own, :] + step_ref[0:1, 0:1] * update
+        new_ref[own, :] = fresh.astype(new_ref.dtype)
+        if not last:
+            attn_in = layer_norm(fresh) * (1.0 + next_ref[1:2, :]) + next_ref[0:1, :]
+            gathered_ref[c, z] = attn_in.astype(jnp.bfloat16)
+            next_gather.start(c)
+
+    stages = [after_attention, feed_forward, after_feed_forward]
+    if not last:
+        stages.append(lambda c: next_gather.forward(c))
+    for tick in range(chunks + len(stages) - 1):
+        for place, stage in enumerate(stages):
+            if 0 <= tick - place < chunks:
+                stage(tick - place)
+    for c in range(chunks):
+        attn_out.finish(c)
+        mlp_gather.finish(c)
+        mlp_out.finish(c)
+        if not last:
+            next_gather.finish(c)
+
+
+def chunk_count(tokens):
+    return max(1, min(2, tokens // 16))
+
+
+def block_tail(n, last, step_size, mixed, out_weight, latent, mods, next_mods, fc_in, fc_out):
+    tokens, width = latent.shape
+    chunks = chunk_count(tokens)
+    rows = tokens // chunks
+    blocks = (chunks, n, rows, width)
+    vmem = pl.BlockSpec(memory_space=pltpu.VMEM)
+    gathered_shape = (8, 128) if last else blocks
+    dma = pltpu.SemaphoreType.DMA
+    return pl.pallas_call(
+        functools.partial(tail_kernel, n, chunks, last),
+        out_shape=(
+            jax.ShapeDtypeStruct((tokens, width), jnp.bfloat16 if last else jnp.float32),
+            jax.ShapeDtypeStruct((tokens, width), jnp.bfloat16),
+            jax.ShapeDtypeStruct(gathered_shape, jnp.bfloat16),
+        ),
+        in_specs=[vmem] * 8,
+        out_specs=(vmem, vmem, vmem),
+        scratch_shapes=[
+            pltpu.VMEM(blocks, jnp.bfloat16),
+            pltpu.VMEM((2,) + blocks, jnp.bfloat16),
+            pltpu.VMEM(blocks, jnp.bfloat16),
+            pltpu.VMEM(blocks, jnp.bfloat16),
+            pltpu.VMEM((2,) + blocks, jnp.bfloat16),
+            pltpu.VMEM((chunks, rows, width), jnp.float32),
+            pltpu.VMEM((rows, width), jnp.float32),
+            pltpu.VMEM((n * rows, fc_in.shape[1]), jnp.bfloat16),
+            dma((chunks, n)),
+            dma((2, chunks, n)),
+            dma((2, chunks, n)),
+            dma((chunks, n)),
+            dma((chunks, n)),
+            dma((2, chunks, n)),
+            dma((2, chunks, n)),
+            dma((chunks, n)),
+        ],
+        compiler_params=pltpu.CompilerParams(
+            collective_id=1 if last else 0,
+            has_side_effects=True,
+            vmem_limit_bytes=48 * 1024 * 1024,
+        ),
+        cost_estimate=pl.CostEstimate(
+            flops=4 * n * tokens * width * fc_in.shape[1],
+            bytes_accessed=4 * width * fc_in.shape[1],
+            transcendentals=n * tokens * fc_in.shape[1],
+        ),
+    )(step_size, mixed, out_weight, latent, mods, next_mods, fc_in, fc_out)
 
 
 def shards(
@@ -51,8 +371,7 @@
     )
     mod_part = jnp.einsum("sf,fkd->skd", embedding, mod_weight, preferred_element_type=jnp.float32)
     modulation = lax.all_gather(mod_part, "tensor", axis=2, tiled=True)
-    block_rows = lax.all_gather(delta_values, "tensor", axis=1, tiled=True)
-    own_delta = lax.dynamic_slice_in_dim(block_rows, column_index * head_width, head_width, 2)
+    own_delta = lax.all_to_all(delta_values, "tensor", split_axis=2, concat_axis=1, tiled=True)
     own_scales = lax.dynamic_slice_in_dim(delta_scales, column_index * heads_here, heads_here, 2)
     row_scales = jnp.repeat(own_scales, head_dim, axis=1)
     dequantize_piece = lax.all_gather(own_delta, "fsdp", axis=1, tiled=True)
@@ -67,10 +386,15 @@
     text_k = text_keys[0]
     text_v = text_values[0]
     velocities = []
+    n = lax.axis_size("tensor")
+    width = latent.shape[1]
+    chunks = chunk_count(latent.shape[0])
+    first = modulation[0]
+    attn_in = (layer_norm(latent) * (1.0 + first[1]) + first[0]).astype(jnp.bfloat16)
+    piece = lax.all_gather(attn_in, "tensor", axis=0, tiled=True)
+    piece = piece.reshape(n, chunks, -1, width).swapaxes(0, 1).reshape(-1, width)
     for step in range(STEPS):
         mods = modulation[step]
-        attn_in = (layer_norm(latent) * (1.0 + mods[1]) + mods[0]).astype(jnp.bfloat16)
-        piece = lax.all_gather(attn_in, "tensor", axis=0, tiled=True)
         count = piece.shape[0]
         joined = jnp.einsum("rd,kdc->rkc", piece, qkv_weights, preferred_element_type=jnp.float32)
         query = rms_scale(joined[:, 0].reshape(count, heads_here, head_dim), q_gain).reshape(
@@ -98,35 +422,24 @@
             "hqk,khd->qhd", soft, all_values, preferred_element_type=jnp.float32
         ).astype(jnp.bfloat16)
         mixed = mixed.reshape(video_count, head_width)
-        attn = lax.psum_scatter(
-            lax.dot_general(
-                mixed, out_weight, (((1,), (1,)), ((), ())), preferred_element_type=jnp.float32
-            ).astype(jnp.bfloat16),
-            "tensor",
-            scatter_dimension=0,
-            tiled=True,
-        ).astype(jnp.float32)
-        midway = latent + mods[2] * attn
-        mlp_in = (layer_norm(midway) * (1.0 + mods[4]) + mods[3]).astype(jnp.bfloat16)
-        hidden = jax.nn.gelu(
-            jnp.dot(
-                lax.all_gather(mlp_in, "tensor", axis=0, tiled=True),
-                fc_in,
-                preferred_element_type=jnp.float32,
-            ),
-            approximate=True,
-        ).astype(jnp.bfloat16)
-        mlp = lax.psum_scatter(
-            jnp.dot(hidden, fc_out, preferred_element_type=jnp.float32).astype(jnp.bfloat16),
-            "tensor",
-            scatter_dimension=0,
-            tiled=True,
-        ).astype(jnp.float32)
-        update = mods[2] * attn + mods[5] * mlp
-        velocities.append(update.astype(jnp.bfloat16))
         step_size = (timesteps[0, step + 1] - timesteps[0, step]).astype(jnp.float32) / 1000.0
-        latent = latent + step_size * update
-    return (latent.astype(jnp.bfloat16)[None], jnp.stack(velocities)[None])
+        last = step == STEPS - 1
+        latent, velocity, gathered = block_tail(
+            n,
+            last,
+            step_size.reshape(1, 1),
+            mixed,
+            out_weight,
+            latent,
+            mods,
+            mods if last else modulation[step + 1],
+            fc_in,
+            fc_out,
+        )
+        velocities.append(velocity)
+        if not last:
+            piece = gathered.reshape(-1, width)
+    return (latent[None], jnp.stack(velocities)[None])
 
 
 def solution(mesh):

time: 449 us -> 347 us (0.77)
  waiting for transfers between devices: 353 us -> 21.3 us
  Pallas kernels: 0 us -> 216 us
  blocking collectives: 13.6 us -> 66.2 us
  matrix products: 30.4 us -> 3.67 us
  other arithmetic: 26.3 us -> 10.8 us
    pallas_call x0 -> x2, Pallas kernels: none -> 216 us  [block_tail(): pl.pallas_call(functools.partial(tail_kernel, n, chunks, last), out_shape...]
    all_gather x3 -> x0, waiting for transfers between devices: 140 us -> none  [the longest x2 72.1 us: shards(): lax.all_gather(mlp_in, 'tensor', axis=0, tiled=True)]
    reduce_scatter x4 -> x0, waiting for transfers between devices: 134 us -> none  [the longest x2 68.5 us: shards(): lax.psum_scatter(lax.dot_general(mixed, out_weight, (((1,), (1,)), ((), (...]
    all_gather x2 -> x1, waiting for transfers between devices: 69.3 us -> 0.02 us  [shards(): piece = lax.all_gather(attn_in, 'tensor', axis=0, tiled=True)]
    all_to_all x0 -> x1, blocking collectives: none -> 50.8 us  [shards(): lax.all_to_all(delta_values, 'tensor', split_axis=2, concat_axis=1, tiled...]
    dot_general x4 -> x2, matrix products: 22.2 us -> 0.6 us  [shards(): jnp.einsum('hqk,khd->qhd', soft, all_values, preferred_element_type=jnp.f...]
    all_gather x1, waiting for transfers between devices: 9.47 us -> 21.3 us  [shards(): dequantize_piece = lax.all_gather(own_delta, 'fsdp', axis=1, tiled=True)]
    convert_element_type x4 -> x2, other arithmetic: 6.57 us -> 2.01 us  [the longest x1 1.05 us: shards(): latent = video[0].astype(jnp.float32)]
  transfers between devices with their start and end apart: 10 -> 2, of which waited for: 10 -> 1; matrix products, arithmetic and copies ran while one was open for 2% -> 3% of each run, Pallas kernels for 0% -> 0%
where the time goes in v1:
time: 347 us; the launch traced here: 346 us
  Pallas kernels  216 us (62%)
  blocking collectives  66.2 us (19%)
  waiting for transfers between devices  21.3 us (6%)
  between operations  17.6 us (5%)
  other arithmetic  10.8 us (3%)
  local copies, waits for them, and re-layouts  10.2 us (3%)
  matrix products  3.67 us (1%)
    pallas_call x2, Pallas kernels, block_tail(): pl.pallas_call(functools.partial(tail_kernel, n, chunks, last), out_shape...  216 us
    all_to_all x1, blocking collectives, shards(): lax.all_to_all(delta_values, 'tensor', split_axis=2, concat_axis=1, tiled...  50.8 us
    all_gather x1, waiting for transfers between devices, shards(): dequantize_piece = lax.all_gather(own_delta, 'fsdp', axis=1, tiled=True)  21.3 us
    all_gather x1, blocking collectives, shards(): modulation = lax.all_gather(mod_part, 'tensor', axis=2, tiled=True)  15.5 us
  transfers between devices with their start and end apart: 2, of which 1 were waited for; matrix products, arithmetic and copies ran while one was open for 3% of the time, Pallas kernels for 0%

profile of v1, /device:TPU:0, one launch (start us, length us, event | category | flops | bytes accessed | tf_op | source)
XLA Modules:
  0.0 346.2 jit_solution(4734002263319700314)
XLA Ops:
  7.2 0.0 copy-start
  7.2 0.0 copy-start.1
  7.2 0.0 copy-start.4
  7.2 0.0 all-gather.3.cloned.1.call-start
  7.3 0.8 convert_bitcast_fusion.1
  8.1 0.1 multiply_cosine_fusion
  8.2 0.7 copy-done
  8.9 0.4 fusion.27
  9.3 15.5 %all_gather.9 = f32[2,6,3072]{2,1,0:T(8,128)S(1)} all-gather(f32[2,6,768]{2,1,0:T(8,128)S(1)} %copy.20), channel_id=1, replica_groups=mesh['groups'=2,'fsdp'=4,'tensor'=4] {'tensor'}, dimensions={2}, use_global_device_ids=true | all-gather | bytes 184320 | tf_op jit(solution)/shard_map/all_gather | solution.py:373
  24.7 0.0 copy-start.3
  24.7 0.7 copy-done.3
  25.4 1.1 convert_reduce_fusion
  26.6 0.0 copy-done.1
  26.6 0.3 multiply_reduce_fusion
  26.9 1.0 add_convert_fusion.1
  27.8 0.0 all-gather.3.cloned.1.call-update
  27.9 0.0 copy-start.5
  27.9 0.0 all-gather.5.cloned.1.call-start
  27.9 0.0 copy-done.4
  27.9 1.4 copy.22
  29.4 50.8 %all_to_all.18 = bf16[4,192,512]{1,0,2:T(4,128)(2,1)S(1)} all-to-all(bf16[4,192,512]{1,0,2:T(4,128)(2,1)} %copy.22), channel_id=1, replica_groups=mesh['groups'=2,'fsdp'=4,'tensor'=4] {'tensor'}, dimensions={2} | all-to-all | bytes 1572864 | tf_op jit(solution)/shard_map/all_to_all | solution.py:374
  80.1 1.4 copy.23
  81.5 0.0 all-gather.5.cloned.1.call-update
  81.6 0.7 constant_dynamic-slice_fusion
  82.3 0.1 broadcast_bitcast_fusion
  83.0 0.0 copy-done.5
  83.0 0.7 fusion.36
  86.3 1.0 slice_bitcast_fusion.1
  87.3 1.1 convert_bitcast_fusion.latent_ref
  88.3 0.0 all-gather.3.cloned.1.call-done
  88.3 2.7 copy.21
  91.1 21.3 %all-gather.5.cloned.1.call-done = bf16[4,3072,128]{2,1,0:T(8,128)(2,1)} async-done(((bf16[4,768,128]{2,1,0:T(8,128)(2,1)}), bf16[4,3072,128]{2,1,0:T(8,128)(2,1)}) %all-gather.5.cloned.1.call-update) | async-done | bytes 3145744 | tf_op jit(solution)/shard_map/all_gather | solution.py:377
  112.3 0.0 copy-start.2
  112.4 4.5 %add_convert_fusion = bf16[4,3072,128]{2,1,0:T(8,128)(2,1)S(1)} fusion(bf16[4,3072,128]{2,1,0:T(8,128)(2,1)} %all-gather.5.cloned.1.call-done, bf16[4,3072,128]{2,1,0:T(8,128)(2,1)} %param.18, f32[4,3072]{1,0:T(4,128)S(1)} %bitcast.88), kind=kLoop, calls=%fused_computation | loop fusion | flops 7864320 | bytes 9486336 | tf_op jit(solution)/shard_map/convert_element_type | solution.py:381
  116.8 0.0 copy-done.2
  116.8 0.0 copy-start.6
  116.8 0.0 copy-start.7
  116.9 0.0 copy-start.9
  116.9 1.0 fusion.2
  117.8 0.0 copy-start.8
  117.9 0.1 multiply_reduce_fusion.4
  118.0 0.1 slice_bitcast_fusion.out_weight_ref
  118.1 0.0 copy-done.6
  118.1 0.1 fusion.16
  118.2 0.0 copy-done.7
  118.2 0.0 copy-done.9
  118.2 0.4 fusion.37
  118.6 0.2 fusion.8
  118.8 0.0 copy-done.8
  118.8 0.3 fusion.6.mixed_ref
  119.1 127.5 %shard_map.140 = (f32[64,3072]{1,0:T(8,128)S(1)}, bf16[64,3072]{1,0:T(8,128)(2,1)S(1)}, bf16[2,4,32,3072]{3,2,1,0:T(8,128)(2,1)S(1)}) custom-call(f32[1,1]{1,0:T(1,128)S(6)} %div.59.step_ref, bf16[256,128]{1,0:T(8,128)(2,1)S(1)} %fusion.6.mixed_ref, bf16[3072,128]{1,0:T(8,128)(2,1)S(1)} %slice_bitcast_fusion.out_weight_ref, ...), custom_call_target="tpu_custom_call" | custom-call | flops 2013265920 | bytes 7864320 | tf_op jit(solution)/shard_map/pallas_call | solution.py:309
  246.6 1.0 fusion
  247.6 0.1 multiply_reduce_fusion.2
  247.8 0.1 fusion.19
  247.9 0.4 fusion.38
  248.2 0.2 fusion.9
  248.5 0.3 fusion.7.mixed_ref
  248.8 88.9 %shard_map.141 = (bf16[64,3072]{1,0:T(8,128)(2,1)S(1)}, bf16[64,3072]{1,0:T(8,128)(2,1)S(1)}, bf16[8,128]{1,0:T(8,128)(2,1)}) custom-call(f32[1,1]{1,0:T(1,128)S(6)} %div.58.step_ref, bf16[256,128]{1,0:T(8,128)(2,1)S(1)} %fusion.7.mixed_ref, bf16[3072,128]{1,0:T(8,128)(2,1)S(1)} %slice_bitcast_fusion.out_weight_ref, ...), custom_call_target="tpu_custom_call" | custom-call | flops 2013265920 | bytes 7864320 | tf_op jit(solution)/shard_map/pallas_call | solution.py:309
  337.7 0.9 maximum_bitcast_fusion
  338.7 0.7 copy.33
  (13 shorter events, 0.1 us)
Async XLA Ops:
  7.2 1.7 copy-start
  7.2 19.4 %copy-start.1 = (bf16[1,64,3072]{2,1,0:T(8,128)(2,1)S(1)}, bf16[1,64,3072]{2,1,0:T(8,128)(2,1)}, u32[]{:S(2)}) copy-start(bf16[1,64,3072]{2,1,0:T(8,128)(2,1)} %param.13) | copy-start | bytes 1179652
  7.2 20.7 %copy-start.4 = (bf16[4,192,512]{2,1,0:T(8,128)(2,1)S(1)}, bf16[4,192,512]{2,1,0:T(8,128)(2,1)}, u32[]{:S(2)}) copy-start(bf16[4,192,512]{2,1,0:T(8,128)(2,1)} %param.19) | copy-start | bytes 2359300
  7.2 81.1 %all-gather.3.cloned.1.call-start = ((), (), s32[]{:S(2)}) async-start(), calls=%async_computation.1 | async-start | bytes 1966080 | tf_op jit(solution)/shard_map/all_gather | solution.py:394
  24.7 0.7 copy-start.3
  27.9 55.2 %copy-start.5 = (s32[1,3]{1,0:T(1,128)S(1)}, s32[1,3]{1,0:T(1,128)}, u32[]{:S(2)}) copy-start(s32[1,3]{1,0:T(1,128)} %param.14) | copy-start | bytes 40
  27.9 84.5 %all-gather.5.cloned.1.call-start = ((), (), s32[]{:S(2)}) async-start(), calls=%async_computation.2 | async-start | bytes 3932160 | tf_op jit(solution)/shard_map/all_gather | solution.py:377
  112.3 4.5 %copy-start.2 = (bf16[2,4,32,3072]{3,2,1,0:T(8,128)(2,1)S(1)}, bf16[2,4,32,3072]{3,2,1,0:T(8,128)(2,1)}, u32[]{:S(2)}) copy-start(bf16[2,4,32,3072]{3,2,1,0:T(8,128)(2,1)} %copy.21) | copy-start | bytes 4718596
  116.8 1.3 copy-start.6
  116.8 1.4 copy-start.7
  116.9 1.4 copy-start.9
  117.8 1.0 copy-start.8
Sparse Core Ops, SparseCore 0:
  28.0 54.4 all-gather.2
  84.7 27.6 all-gather.4

commit v2 on v1

--- a/solution.py
+++ b/solution.py
@@ -346,6 +346,203 @@
     )(step_size, mixed, out_weight, latent, mods, next_mods, fc_in, fc_out)
 
 
+def mesh_copy(src, dst, send_sem, recv_sem, axis, target):
+    return pltpu.make_async_remote_copy(
+        src_ref=src,
+        dst_ref=dst,
+        send_sem=send_sem,
+        recv_sem=recv_sem,
+        device_id={axis: target},
+        device_id_type=pl.DeviceIdType.MESH,
+    )
+
+
+def head_kernel(
+    n,
+    owners,
+    chunks,
+    mod_ref,
+    video_ref,
+    delta_ref,
+    modulation_ref,
+    gathered_ref,
+    pieces_ref,
+    mod_all,
+    own_sem,
+    mod_send,
+    mod_recv,
+    line_send,
+    line_recv,
+    chip_send,
+    chip_recv,
+    twin_send,
+    twin_recv,
+    ag_send,
+    ag_recv,
+):
+    z = lax.axis_index("tensor")
+    f = lax.axis_index("fsdp")
+    chip = f // 2
+    core = f - 2 * chip
+    twin = 2 * chip + 1 - core
+    chips = owners // 2
+    tokens, width = video_ref.shape
+    rows = tokens // chunks
+    head_width = pieces_ref.shape[3]
+    barrier = pltpu.get_barrier_semaphore()
+
+    def greet(axis, target):
+        pl.semaphore_signal(
+            barrier, inc=1, device_id={axis: target}, device_id_type=pl.DeviceIdType.MESH
+        )
+
+    for d in range(1, n):
+        greet("tensor", lax.rem(z + d, n))
+    greet("fsdp", twin)
+    for d in range(1, chips):
+        greet("fsdp", 2 * lax.rem(chip + d, chips) + core)
+    pl.semaphore_wait(barrier, n - 1 + chips)
+
+    def mod_copy(owner, d):
+        return mesh_copy(
+            mod_ref,
+            mod_all.at[owner],
+            mod_send.at[d],
+            mod_recv.at[owner],
+            "tensor",
+            lax.rem(z + d, n),
+        )
+
+    def columns(target):
+        return delta_ref.at[:, :, pl.ds(pl.multiple_of(target * head_width, head_width), head_width)]
+
+    def line_piece(owner, d):
+        target = lax.rem(z + d, n)
+        return mesh_copy(
+            columns(target),
+            pieces_ref.at[f * n + owner],
+            line_send.at[d],
+            line_recv.at[owner],
+            "tensor",
+            target,
+        )
+
+    def chip_piece(source, t, d):
+        piece = pieces_ref.at[source * n + t]
+        return mesh_copy(
+            piece,
+            piece,
+            chip_send.at[d, t],
+            chip_recv.at[source, t],
+            "fsdp",
+            2 * lax.rem(chip + d, chips) + core,
+        )
+
+    def twin_piece(source, t):
+        piece = pieces_ref.at[source * n + t]
+        return mesh_copy(
+            piece, piece, twin_send.at[source, t], twin_recv.at[source, t], "fsdp", twin
+        )
+
+    def spread(t):
+        for d in range(1, chips):
+            chip_piece(f, t, d).start()
+        twin_piece(f, t).start()
+
+    for d in range(1, n):
+        mod_copy(z, d).start()
+    own = pltpu.make_async_copy(columns(z), pieces_ref.at[f * n + z], own_sem)
+    own.start()
+    for d in range(1, n):
+        line_piece(z, d).start()
+    mod_all[z] = mod_ref[...]
+    own.wait()
+    spread(z)
+    for d in range(1, n):
+        mod_copy(lax.rem(z + d, n), d).wait_recv()
+    share = mod_ref.shape[1]
+    for t in range(n):
+        modulation_ref[:, t * share : (t + 1) * share] = mod_all[t]
+
+    gather = Gather(z, n, gathered_ref, ag_send, ag_recv)
+    for c in range(chunks):
+        values = video_ref[c * rows : (c + 1) * rows, :].astype(jnp.float32)
+        attn_in = layer_norm(values) * (1.0 + modulation_ref[1:2, :]) + modulation_ref[0:1, :]
+        gathered_ref[c, z] = attn_in.astype(jnp.bfloat16)
+        gather.start(c)
+
+    for d in range(1, n):
+        owner = lax.rem(z + d, n)
+        line_piece(owner, d).wait_recv()
+        spread(owner)
+
+    def arrive(k):
+        for d in range(1, chips):
+            source = 2 * lax.rem(chip + d, chips) + core
+            t = lax.rem(z + k, n)
+            chip_piece(source, t, d).wait_recv()
+            twin_piece(source, t).start()
+
+    steps = n // chunks
+    for c in range(chunks):
+        gather.forward(c)
+        for k in range(c * steps, n if c == chunks - 1 else (c + 1) * steps):
+            arrive(k)
+    for c in range(chunks):
+        gather.finish(c)
+    for j in range(chips):
+        source = 2 * j + 1 - core
+        for t in range(n):
+            twin_piece(source, t).wait_recv()
+            twin_piece(2 * j + core, t).wait_send()
+    for d in range(1, n):
+        mod_copy(z, d).wait_send()
+        line_piece(z, d).wait_send()
+    for d in range(1, chips):
+        for t in range(n):
+            chip_piece(f, t, d).wait_send()
+
+
+def block_head(n, owners, mod_part, video, delta_values):
+    tokens, width = video.shape
+    mats, piece_rows, columns = delta_values.shape
+    chunks = chunk_count(tokens)
+    vmem = pl.BlockSpec(memory_space=pltpu.VMEM)
+    dma = pltpu.SemaphoreType.DMA
+    return pl.pallas_call(
+        functools.partial(head_kernel, n, owners, chunks),
+        out_shape=(
+            jax.ShapeDtypeStruct((mod_part.shape[0], width), jnp.float32),
+            jax.ShapeDtypeStruct((chunks, n, tokens // chunks, width), jnp.bfloat16),
+            jax.ShapeDtypeStruct((owners * n, mats, piece_rows, columns // n), jnp.bfloat16),
+        ),
+        in_specs=[vmem] * 3,
+        out_specs=(vmem, vmem, vmem),
+        scratch_shapes=[
+            pltpu.VMEM((n,) + mod_part.shape, jnp.float32),
+            dma(()),
+            dma((n,)),
+            dma((n,)),
+            dma((n,)),
+            dma((n,)),
+            dma((max(owners // 2, 1), n)),
+            dma((owners, n)),
+            dma((owners, n)),
+            dma((owners, n)),
+            dma((2, chunks, n)),
+            dma((chunks, n)),
+        ],
+        compiler_params=pltpu.CompilerParams(
+            collective_id=2,
+            has_side_effects=True,
+            vmem_limit_bytes=40 * 1024 * 1024,
+        ),
+        cost_estimate=pl.CostEstimate(
+            flops=10 * tokens * width, bytes_accessed=8 * tokens * n * width, transcendentals=0
+        ),
+    )(mod_part, video, delta_values)
+
+
 def shards(
     video,
     timesteps,
@@ -370,11 +567,17 @@
         jnp.bfloat16
     )
     mod_part = jnp.einsum("sf,fkd->skd", embedding, mod_weight, preferred_element_type=jnp.float32)
-    modulation = lax.all_gather(mod_part, "tensor", axis=2, tiled=True)
-    own_delta = lax.all_to_all(delta_values, "tensor", split_axis=2, concat_axis=1, tiled=True)
+    n = lax.axis_size("tensor")
+    owners = lax.axis_size("fsdp")
+    width = video.shape[2]
+    modulation, piece, delta_pieces = block_head(
+        n, owners, mod_part.reshape(-1, mod_part.shape[2]), video[0], delta_values
+    )
+    modulation = modulation.reshape(STEPS, -1, width)
+    piece = piece.reshape(-1, width)
     own_scales = lax.dynamic_slice_in_dim(delta_scales, column_index * heads_here, heads_here, 2)
     row_scales = jnp.repeat(own_scales, head_dim, axis=1)
-    dequantize_piece = lax.all_gather(own_delta, "fsdp", axis=1, tiled=True)
+    dequantize_piece = delta_pieces.swapaxes(0, 1).reshape(base_weights.shape)
     scale_full = jnp.repeat(row_scales, head_dim, axis=2)
     weights = (
         base_weights.astype(jnp.float32) + dequantize_piece.astype(jnp.float32) * scale_full
@@ -386,13 +589,6 @@
     text_k = text_keys[0]
     text_v = text_values[0]
     velocities = []
-    n = lax.axis_size("tensor")
-    width = latent.shape[1]
-    chunks = chunk_count(latent.shape[0])
-    first = modulation[0]
-    attn_in = (layer_norm(latent) * (1.0 + first[1]) + first[0]).astype(jnp.bfloat16)
-    piece = lax.all_gather(attn_in, "tensor", axis=0, tiled=True)
-    piece = piece.reshape(n, chunks, -1, width).swapaxes(0, 1).reshape(-1, width)
     for step in range(STEPS):
         mods = modulation[step]
         count = piece.shape[0]

time: 347 us -> 296 us (0.85)
  blocking collectives: 66.2 us -> 0 us
  Pallas kernels: 216 us -> 272 us
  waiting for transfers between devices: 21.3 us -> 0 us
  between operations: 17.6 us -> 4.25 us
    pallas_call x0 -> x1, Pallas kernels: none -> 55.2 us  [block_head(): pl.pallas_call(functools.partial(head_kernel, n, owners, chunks), out_sha...]
    all_to_all x1 -> x0, blocking collectives: 50.8 us -> none  [shards(): lax.all_to_all(delta_values, 'tensor', split_axis=2, concat_axis=1, tiled...]
    all_gather x2 -> x0, waiting for transfers between devices: 21.3 us -> none  [the longest x1 21.3 us: shards(): dequantize_piece = lax.all_gather(own_delta, 'fsdp', axis=1, tiled=True)]
    all_gather x1 -> x0, blocking collectives: 15.5 us -> none  [shards(): modulation = lax.all_gather(mod_part, 'tensor', axis=2, tiled=True)]
  transfers between devices with their start and end apart: 2 -> 0, of which waited for: 1 -> 0; matrix products, arithmetic and copies ran while one was open for 3% -> 0% of each run, Pallas kernels for 0% -> 0%
where the time goes in v2:
time: 296 us
  Pallas kernels  272 us (92%)
  other arithmetic  8.73 us (3%)
  local copies, waits for them, and re-layouts  7.61 us (3%)
  between operations  4.25 us (1%)
  matrix products  3.66 us (1%)
    pallas_call x2, Pallas kernels, block_tail(): pl.pallas_call(functools.partial(tail_kernel, n, chunks, last), out_shape...  216 us
    pallas_call x1, Pallas kernels, block_head(): pl.pallas_call(functools.partial(head_kernel, n, owners, chunks), out_sha...  55.2 us

profile of v2, /device:TPU:0, one launch (start us, length us, event | category | flops | bytes accessed | tf_op | source)
XLA Modules:
  0.0 295.8 jit_solution(16727743236569485137)
XLA Ops:
  0.6 0.0 copy-start
  0.6 0.0 copy-start.3
  0.7 1.5 fusion.39
  4.8 0.7 convert_bitcast_fusion.1
  5.5 0.1 multiply_cosine_fusion
  5.6 0.0 copy-done
  5.6 0.4 fusion.29
  6.0 0.0 copy-done.3
  6.0 0.0 copy-start.1
  6.1 1.0 copy-done.1
  7.0 55.2 %shard_map.140 = (f32[12,3072]{1,0:T(8,128)S(1)}, bf16[2,4,32,3072]{3,2,1,0:T(8,128)(2,1)S(1)}, bf16[16,4,192,128]{3,2,1,0:T(8,128)(2,1)S(1)}) custom-call(f32[12,768]{1,0:T(8,128)S(1)} %reshape.179.mod_ref, bf16[64,3072]{1,0:T(8,128)(2,1)S(1)} %bitcast.71, bf16[4,192,512]{2,1,0:T(8,128)(2,1)S(1)} %copy-done.3), custom_call_target="tpu_custom_call" | custom-call | flops 1966080 | bytes 6291456 | tf_op jit(solution)/shard_map/pallas_call | solution.py:512
  62.2 0.0 copy-start.4
  62.2 0.8 convert_bitcast_fusion
  63.0 0.3 copy-done.4
  63.4 3.1 %copy.20 = f32[4,16,192,128]{3,2,1,0:T(8,128)} copy(f32[4,16,192,128]{3,2,0,1:T(8,128)S(1)} %convert_bitcast_fusion) | data formatting | bytes 12582912 | tf_op jit(solution)/shard_map/convert_element_type | solution.py:583
  66.4 0.7 constant_dynamic-slice_fusion
  67.1 0.1 broadcast_bitcast_fusion
  67.2 0.0 copy-start.5
  67.2 5.2 %fusion.1 = bf16[4,3072,128]{2,1,0:T(8,128)(2,1)S(1)} fusion(f32[4,16,192,128]{3,2,1,0:T(8,128)} %copy.20, bf16[4,3072,128]{2,1,0:T(8,128)(2,1)} %param.18, f32[4,3072]{1,0:T(4,128)S(1)} %bitcast.77), kind=kLoop, calls=%fused_computation.2 | loop fusion | flops 6291456 | bytes 12632064 | tf_op jit(solution)/shard_map/convert_element_type | solution.py:584
  72.4 0.0 copy-done.5
  72.4 0.0 copy-start.6
  72.4 0.0 copy-start.7
  72.5 0.0 copy-start.9
  72.5 0.0 copy-start.8
  72.5 1.0 fusion.4
  73.5 0.0 copy-start.2
  73.5 0.1 multiply_reduce_fusion.3
  73.6 0.0 copy-done.6
  73.6 0.1 fusion.18
  74.4 0.0 copy-done.7
  74.4 0.0 copy-done.9
  74.4 0.4 fusion.40
  74.8 0.2 fusion.10
  75.0 0.0 copy-done.8
  75.1 0.3 fusion.8.mixed_ref
  75.4 0.1 slice_bitcast_fusion.out_weight_ref
  75.4 0.0 copy-done.2
  75.4 0.1 bitcast_convert_fusion.latent_ref
  75.5 128.1 %shard_map.141 = (f32[64,3072]{1,0:T(8,128)S(1)}, bf16[64,3072]{1,0:T(8,128)(2,1)S(1)}, bf16[2,4,32,3072]{3,2,1,0:T(8,128)(2,1)S(1)}) custom-call(f32[1,1]{1,0:T(1,128)S(6)} %div.53.step_ref, bf16[256,128]{1,0:T(8,128)(2,1)S(1)} %fusion.8.mixed_ref, bf16[3072,128]{1,0:T(8,128)(2,1)S(1)} %slice_bitcast_fusion.out_weight_ref, ...), custom_call_target="tpu_custom_call" | custom-call | flops 2013265920 | bytes 7864320 | tf_op jit(solution)/shard_map/pallas_call | solution.py:309
  203.6 1.0 fusion.2
  204.6 0.1 multiply_reduce_fusion.1
  204.8 0.1 fusion.21
  204.9 0.4 fusion.41
  205.3 0.2 fusion.11
  205.5 0.3 fusion.9.mixed_ref
  205.8 88.3 %shard_map.142 = (bf16[64,3072]{1,0:T(8,128)(2,1)S(1)}, bf16[64,3072]{1,0:T(8,128)(2,1)S(1)}, bf16[8,128]{1,0:T(8,128)(2,1)}) custom-call(f32[1,1]{1,0:T(1,128)S(6)} %div.52.step_ref, bf16[256,128]{1,0:T(8,128)(2,1)S(1)} %fusion.9.mixed_ref, bf16[3072,128]{1,0:T(8,128)(2,1)S(1)} %slice_bitcast_fusion.out_weight_ref, ...), custom_call_target="tpu_custom_call" | custom-call | flops 2013265920 | bytes 7864320 | tf_op jit(solution)/shard_map/pallas_call | solution.py:309
  294.1 0.9 maximum_bitcast_fusion
  295.0 0.7 copy.30
  (12 shorter events, 0.1 us)
Async XLA Ops:
  0.6 5.0 %copy-start = (bf16[256,6,768]{2,0,1:T(8,128)(2,1)S(1)}, bf16[256,6,768]{2,0,1:T(8,128)(2,1)}, u32[]{:S(2)}) copy-start(bf16[256,6,768]{2,0,1:T(8,128)(2,1)} %param.23) | copy-start | bytes 7077892
  0.6 5.4 %copy-start.3 = (bf16[4,192,512]{2,1,0:T(8,128)(2,1)S(1)}, bf16[4,192,512]{2,1,0:T(8,128)(2,1)}, u32[]{:S(2)}) copy-start(bf16[4,192,512]{2,1,0:T(8,128)(2,1)} %delta_ref.1) | copy-start | bytes 2359300
  6.0 1.0 copy-start.1
  62.2 1.1 copy-start.4
  67.2 5.2 %copy-start.5 = (bf16[2,4,32,3072]{3,2,1,0:T(8,128)(2,1)S(1)}, bf16[2,4,32,3072]{3,2,1,0:T(8,128)(2,1)}, u32[]{:S(2)}) copy-start(bf16[2,4,32,3072]{3,2,1,0:T(8,128)(2,1)} %copy-done.4) | copy-start | bytes 4718596
  72.4 1.2 copy-start.6
  72.4 2.0 copy-start.7
  72.5 2.0 copy-start.9
  72.5 2.6 copy-start.8
  73.5 2.0 copy-start.2

commit v3 on v2

--- a/solution.py
+++ b/solution.py
@@ -55,7 +55,11 @@
             barrier, inc=1, device_id={"tensor": z + 1}, device_id_type=pl.DeviceIdType.MESH
         )
 
-    pl.semaphore_wait(barrier, jnp.where(z > 0, 1, 0) + jnp.where(z < n - 1, 1, 0))
+
+def await_neighbours(z, n):
+    pl.semaphore_wait(
+        pltpu.get_barrier_semaphore(), jnp.where(z > 0, 1, 0) + jnp.where(z < n - 1, 1, 0)
+    )
 
 
 class Gather:
@@ -80,25 +84,25 @@
         def _():
             self.copy(c, z, 1).start()
 
-    def forward(self, c):
+    def forward(self, c, k):
         z, n = self.z, self.n
-        for d in range(1, n):
-
-            @pl.when(z - d >= 0)
-            def _():
-                self.copy(c, z - d, 0).wait_recv()
-
-                @pl.when(z < n - 1)
-                def _():
-                    self.copy(c, z - d, 0).start()
-
-            @pl.when(z + d <= n - 1)
-            def _():
-                self.copy(c, z + d, 1).wait_recv()
-
-                @pl.when(z > 0)
-                def _():
-                    self.copy(c, z + d, 1).start()
+        d = k + 1
+
+        @pl.when(z - d >= 0)
+        def _():
+            self.copy(c, z - d, 0).wait_recv()
+
+            @pl.when(z < n - 1)
+            def _():
+                self.copy(c, z - d, 0).start()
+
+        @pl.when(z + d <= n - 1)
+        def _():
+            self.copy(c, z + d, 1).wait_recv()
+
+            @pl.when(z > 0)
+            def _():
+                self.copy(c, z + d, 1).start()
 
     def finish(self, c):
         z, n = self.z, self.n
@@ -146,18 +150,19 @@
         self.term[c, o] = total.astype(jnp.bfloat16)
         self.copy(c, o, way).start()
 
-    def forward(self, c):
+    def forward(self, c, k):
         z, n = self.z, self.n
-        for k in range(n - 1):
-            right, left = n - 1 - k, k
-
-            @pl.when((z > 0) & (z < right))
-            def _():
-                self.add(c, right, 0)
-
-            @pl.when((z < n - 1) & (z > left))
-            def _():
-                self.add(c, left, 1)
+        turn = k + 1
+        if turn == n - 1:
+            return
+
+        @pl.when((z > 0) & (z <= turn))
+        def _():
+            self.add(c, z + n - 1 - turn, 0)
+
+        @pl.when((z < n - 1) & (z >= n - 1 - turn))
+        def _():
+            self.add(c, z - (n - 1 - turn), 1)
 
     def collect(self, c, total):
         z, n = self.z, self.n
@@ -196,8 +201,8 @@
     latent_ref,
     mods_ref,
     next_ref,
-    fc_in_ref,
-    fc_out_ref,
+    fc_in_hbm,
+    fc_out_hbm,
     new_ref,
     velocity_ref,
     gathered_ref,
@@ -209,6 +214,9 @@
     attn_sum,
     total,
     hidden_ref,
+    fc_in_ref,
+    fc_out_ref,
+    load_sem,
     as_send,
     as_recv,
     mg_send,
@@ -228,6 +236,12 @@
     next_gather = None if last else Gather(z, n, gathered_ref, ag_send, ag_recv)
 
     greet_neighbours(z, n)
+    loads = [
+        pltpu.make_async_copy(fc_in_hbm, fc_in_ref, load_sem.at[0]),
+        pltpu.make_async_copy(fc_out_hbm, fc_out_ref, load_sem.at[1]),
+    ]
+    for load in loads:
+        load.start()
     for c in range(chunks):
         part = mixed_ref[c * n * rows : (c + 1) * n * rows, :]
         for t in range(0, width, tile):
@@ -238,10 +252,11 @@
                 preferred_element_type=jnp.float32,
             ).astype(jnp.bfloat16)
             attn_term[c, :, :, t : t + tile] = product.reshape(n, rows, tile)
+    await_neighbours(z, n)
+    for c in range(chunks):
         attn_out.ends(c)
 
     def after_attention(c):
-        attn_out.forward(c)
         attn_out.collect(c, attn_sum.at[c])
         own = slice(c * rows, (c + 1) * rows)
         gated = mods_ref[2:3, :] * attn_sum[c]
@@ -252,7 +267,9 @@
         mlp_gather.start(c)
 
     def feed_forward(c):
-        mlp_gather.forward(c)
+        if c == 0:
+            for load in loads:
+                load.wait()
         tokens_in = mlp_in_all[c].reshape(n * rows, width)
         hidden = jax.nn.gelu(
             jnp.dot(tokens_in, fc_in_ref[...], preferred_element_type=jnp.float32),
@@ -267,7 +284,6 @@
         mlp_out.ends(c)
 
     def after_feed_forward(c):
-        mlp_out.forward(c)
         mlp_out.collect(c, total)
         own = slice(c * rows, (c + 1) * rows)
         update = attn_sum[c] + mods_ref[5:6, :] * total[...]
@@ -279,13 +295,25 @@
             gathered_ref[c, z] = attn_in.astype(jnp.bfloat16)
             next_gather.start(c)
 
-    stages = [after_attention, feed_forward, after_feed_forward]
+    stages = [
+        (attn_out.forward, after_attention),
+        (mlp_gather.forward, feed_forward),
+        (mlp_out.forward, after_feed_forward),
+    ]
     if not last:
-        stages.append(lambda c: next_gather.forward(c))
+        stages.append((next_gather.forward, None))
     for tick in range(chunks + len(stages) - 1):
-        for place, stage in enumerate(stages):
-            if 0 <= tick - place < chunks:
-                stage(tick - place)
+        active = [
+            (tick - place, stage)
+            for place, stage in enumerate(stages)
+            if 0 <= tick - place < chunks
+        ]
+        for k in range(n - 1):
+            for c, stage in active:
+                stage[0](c, k)
+        for c, stage in active:
+            if stage[1] is not None:
+                stage[1](c)
     for c in range(chunks):
         attn_out.finish(c)
         mlp_gather.finish(c)
@@ -313,7 +341,7 @@
             jax.ShapeDtypeStruct((tokens, width), jnp.bfloat16),
             jax.ShapeDtypeStruct(gathered_shape, jnp.bfloat16),
         ),
-        in_specs=[vmem] * 8,
+        in_specs=[vmem] * 6 + [pl.BlockSpec(memory_space=pl.ANY)] * 2,
         out_specs=(vmem, vmem, vmem),
         scratch_shapes=[
             pltpu.VMEM(blocks, jnp.bfloat16),
@@ -324,6 +352,9 @@
             pltpu.VMEM((chunks, rows, width), jnp.float32),
             pltpu.VMEM((rows, width), jnp.float32),
             pltpu.VMEM((n * rows, fc_in.shape[1]), jnp.bfloat16),
+            pltpu.VMEM(fc_in.shape, jnp.bfloat16),
+            pltpu.VMEM(fc_out.shape, jnp.bfloat16),
+            dma((2,)),
             dma((chunks, n)),
             dma((2, chunks, n)),
             dma((2, chunks, n)),
@@ -485,7 +516,8 @@
 
     steps = n // chunks
     for c in range(chunks):
-        gather.forward(c)
+        for k in range(n - 1):
+            gather.forward(c, k)
         for k in range(c * steps, n if c == chunks - 1 else (c + 1) * steps):
             arrive(k)
     for c in range(chunks):

time: 296 us -> 258 us (0.87)
  Pallas kernels: 272 us -> 234 us
    pallas_call x2, Pallas kernels: 216 us -> 179 us  [block_tail(): pl.pallas_call(functools.partial(tail_kernel, n, chunks, last), out_shape...]
where the time goes in v3:
time: 258 us
  Pallas kernels  234 us (91%)
  other arithmetic  8.73 us (3%)
  local copies, waits for them, and re-layouts  7.61 us (3%)
  between operations  4.25 us (2%)
  matrix products  3.66 us (1%)
    pallas_call x2, Pallas kernels, block_tail(): pl.pallas_call(functools.partial(tail_kernel, n, chunks, last), out_shape...  179 us
    pallas_call x1, Pallas kernels, block_head(): pl.pallas_call(functools.partial(head_kernel, n, owners, chunks), out_sha...  55.2 us
    convert_element_type x1, other arithmetic, shards(): weights = (base_weights.astype(jnp.float32) + dequantize_piece.astype(jnp...  5.18 us

profile of v3, /device:TPU:0, one launch (start us, length us, event | category | flops | bytes accessed | tf_op | source)
XLA Modules:
  0.0 258.2 jit_solution(11080623939239226846)
XLA Ops:
  0.6 0.0 copy-start
  0.6 0.0 copy-start.3
  0.7 1.5 fusion.39
  4.8 0.7 convert_bitcast_fusion.1
  5.5 0.1 multiply_cosine_fusion
  5.6 0.0 copy-done
  5.6 0.4 fusion.29
  6.0 0.0 copy-done.3
  6.0 0.0 copy-start.1
  6.1 1.0 copy-done.1
  7.0 55.2 %shard_map.140 = (f32[12,3072]{1,0:T(8,128)S(1)}, bf16[2,4,32,3072]{3,2,1,0:T(8,128)(2,1)S(1)}, bf16[16,4,192,128]{3,2,1,0:T(8,128)(2,1)S(1)}) custom-call(f32[12,768]{1,0:T(8,128)S(1)} %reshape.179.mod_ref, bf16[64,3072]{1,0:T(8,128)(2,1)S(1)} %bitcast.71, bf16[4,192,512]{2,1,0:T(8,128)(2,1)S(1)} %copy-done.3), custom_call_target="tpu_custom_call" | custom-call | flops 1966080 | bytes 6291456 | tf_op jit(solution)/shard_map/pallas_call | solution.py:544
  62.2 0.0 copy-start.4
  62.2 0.8 convert_bitcast_fusion
  63.0 0.3 copy-done.4
  63.4 3.1 %copy.20 = f32[4,16,192,128]{3,2,1,0:T(8,128)} copy(f32[4,16,192,128]{3,2,0,1:T(8,128)S(1)} %convert_bitcast_fusion) | data formatting | bytes 12582912 | tf_op jit(solution)/shard_map/convert_element_type | solution.py:615
  66.4 0.7 constant_dynamic-slice_fusion
  67.1 0.1 broadcast_bitcast_fusion
  67.2 0.0 copy-start.5
  67.2 5.2 %fusion.1 = bf16[4,3072,128]{2,1,0:T(8,128)(2,1)S(1)} fusion(f32[4,16,192,128]{3,2,1,0:T(8,128)} %copy.20, bf16[4,3072,128]{2,1,0:T(8,128)(2,1)} %param.18, f32[4,3072]{1,0:T(4,128)S(1)} %bitcast.77), kind=kLoop, calls=%fused_computation.2 | loop fusion | flops 6291456 | bytes 12632064 | tf_op jit(solution)/shard_map/convert_element_type | solution.py:616
  72.4 0.0 copy-done.5
  72.4 0.0 copy-start.6
  72.4 0.0 copy-start.7
  72.5 0.0 copy-start.9
  72.5 0.0 copy-start.8
  72.5 1.0 fusion.4
  73.5 0.0 copy-start.2
  73.5 0.1 multiply_reduce_fusion.3
  73.6 0.0 copy-done.6
  73.6 0.1 fusion.18
  74.4 0.0 copy-done.7
  74.4 0.0 copy-done.9
  74.4 0.4 fusion.40
  74.8 0.2 fusion.10
  75.0 0.0 copy-done.8
  75.1 0.3 fusion.8.mixed_ref
  75.4 0.1 slice_bitcast_fusion.out_weight_ref
  75.4 0.0 copy-done.2
  75.4 0.1 bitcast_convert_fusion.latent_ref
  75.5 109.9 %shard_map.141 = (f32[64,3072]{1,0:T(8,128)S(1)}, bf16[64,3072]{1,0:T(8,128)(2,1)S(1)}, bf16[2,4,32,3072]{3,2,1,0:T(8,128)(2,1)S(1)}) custom-call(f32[1,1]{1,0:T(1,128)S(6)} %div.53.step_ref, bf16[256,128]{1,0:T(8,128)(2,1)S(1)} %fusion.8.mixed_ref, bf16[3072,128]{1,0:T(8,128)(2,1)S(1)} %slice_bitcast_fusion.out_weight_ref, ...), custom_call_target="tpu_custom_call" | custom-call | flops 2013265920 | bytes 7864320 | tf_op jit(solution)/shard_map/pallas_call | solution.py:337
  185.5 1.0 fusion.2
  186.5 0.1 multiply_reduce_fusion.1
  186.6 0.1 fusion.21
  186.7 0.4 fusion.41
  187.1 0.2 fusion.11
  187.3 0.3 fusion.9.mixed_ref
  187.6 68.9 %shard_map.142 = (bf16[64,3072]{1,0:T(8,128)(2,1)S(1)}, bf16[64,3072]{1,0:T(8,128)(2,1)S(1)}, bf16[8,128]{1,0:T(8,128)(2,1)}) custom-call(f32[1,1]{1,0:T(1,128)S(6)} %div.52.step_ref, bf16[256,128]{1,0:T(8,128)(2,1)S(1)} %fusion.9.mixed_ref, bf16[3072,128]{1,0:T(8,128)(2,1)S(1)} %slice_bitcast_fusion.out_weight_ref, ...), custom_call_target="tpu_custom_call" | custom-call | flops 2013265920 | bytes 7864320 | tf_op jit(solution)/shard_map/pallas_call | solution.py:337
  256.5 0.9 maximum_bitcast_fusion
  257.5 0.7 copy.30
  (12 shorter events, 0.1 us)
Async XLA Ops:
  0.6 5.0 %copy-start = (bf16[256,6,768]{2,0,1:T(8,128)(2,1)S(1)}, bf16[256,6,768]{2,0,1:T(8,128)(2,1)}, u32[]{:S(2)}) copy-start(bf16[256,6,768]{2,0,1:T(8,128)(2,1)} %param.23) | copy-start | bytes 7077892
  0.6 5.4 %copy-start.3 = (bf16[4,192,512]{2,1,0:T(8,128)(2,1)S(1)}, bf16[4,192,512]{2,1,0:T(8,128)(2,1)}, u32[]{:S(2)}) copy-start(bf16[4,192,512]{2,1,0:T(8,128)(2,1)} %delta_ref.1) | copy-start | bytes 2359300
  6.0 1.0 copy-start.1
  62.2 1.1 copy-start.4
  67.2 5.2 %copy-start.5 = (bf16[2,4,32,3072]{3,2,1,0:T(8,128)(2,1)S(1)}, bf16[2,4,32,3072]{3,2,1,0:T(8,128)(2,1)}, u32[]{:S(2)}) copy-start(bf16[2,4,32,3072]{3,2,1,0:T(8,128)(2,1)} %copy-done.4) | copy-start | bytes 4718596
  72.4 1.2 copy-start.6
  72.4 2.0 copy-start.7
  72.5 2.0 copy-start.9
  72.5 2.6 %copy-start.8 = (bf16[1,256,128]{2,1,0:T(8,128)(2,1)S(1)}, bf16[1,256,128]{2,1,0:T(8,128)(2,1)}, u32[]{:S(2)}) copy-start(bf16[1,256,128]{2,1,0:T(8,128)(2,1)} %param.16) | copy-start | bytes 196612
  73.5 2.0 copy-start.2
